TPU v7x, 32 devices: a whole 2x2x4 slice. The times are simulated.
32 devices in a mesh: frame: 16 (over z, x, core), head: 2 (over y).
Axes of the slice: x: 2, y: 2, z: 4, core: 2. Of those that a mesh axis runs over, the one named last changes fastest.
Arguments:
- tokens: bfloat16 [2048, 5120], P('frame'), may hold values from -6 to 6
- w_query: bfloat16 [5120, 3072], P('frame', 'head')
- w_key: bfloat16 [5120, 3072], P('frame', 'head')
- w_value: bfloat16 [5120, 3072], P('frame', 'head'), may hold values from -0.078125 to 0.078125
- query_gain: float32 [3072], P('head')
- key_gain: float32 [3072], P('head')
- key_tiles: int32 [16, 8], replicated, may hold values from -1 to 15, as said below
Outputs:
- attended: bfloat16 [2048, 3072], P('frame', 'head')
Inputs may be any that keep to these rules, and one draw needn't show every extreme that they name: Each frame index holds exactly one query tile, so tile t lives on frame index t. Row t of key_tiles names distinct key tiles first and is padded with -1 after them. A named tile u has u - t in 0, 1, -1, 2, -2 or plus or minus a power of two from 4 up to half the number of frame devices, and every tile with u - t in 0, 1, -1 that exists is named.
All inputs are finite; a program needn't handle non-finite values.
Results may differ from a plain program's by a relative error of at most 0.028.
Values may be sent and summed in bfloat16 or wider, within the bound.
A program may use at most 128 MiB of HBM per device.

v0:
```python
import jax
import jax.numpy as jnp
from jax import lax
from jax.sharding import PartitionSpec as P

HEAD_DIM = 128
HEADS = 24
TILE = 128


def passed_along(value, axis, steps):
    count = lax.axis_size(axis)
    leading, last = (max(0, -steps), min(count, count - steps))
    return lax.ppermute(value, axis, [(source, source + steps) for source in range(leading, last)])


def add_rows(tokens, panel):
    return jnp.dot(tokens, panel, preferred_element_type=jnp.float32)


def rms_scale(values, totals, gain):
    mean_square = totals / (HEADS * HEAD_DIM)
    return (values * lax.rsqrt(mean_square + 1e-06)[:, None] * gain[None, :]).astype(jnp.bfloat16)


def shard_ids(owner, frames, tiles_here):
    inside = (owner >= 0) & (owner < frames)
    tile_range = jnp.arange(tiles_here, dtype=jnp.int32)
    return jnp.where(inside, owner * tiles_here + tile_range, -2)


def requested(entries, owner, tiles_here):
    inside = (entries >= owner * tiles_here) & (entries < (owner + 1) * tiles_here)
    return jnp.max(jnp.where(inside, entries - owner * tiles_here, 0))


def on_device(tokens, w_query, w_key, w_value, query_gain, key_gain, key_tiles):
    frames = lax.axis_size("frame")
    position = lax.axis_index("frame")
    rows_here = tokens.shape[0]
    tiles_here = rows_here // TILE
    columns = w_query.shape[1]
    heads_here = columns // HEAD_DIM

    def add_one(panel):
        return add_rows(tokens, panel)

    query = add_one(lax.all_gather(w_query, "frame", axis=0, tiled=True))
    key_full = add_one(lax.all_gather(w_key, "frame", axis=0, tiled=True))
    value_full = add_one(lax.all_gather(w_value, "frame", axis=0, tiled=True))
    query_total, key_total = lax.psum(
        (jnp.sum(query * query, axis=1), jnp.sum(key_full * key_full, axis=1)), "head"
    )
    query_normed = rms_scale(query, query_total, query_gain)
    key_normed = rms_scale(key_full, key_total, key_gain)
    value_cast = value_full.astype(jnp.bfloat16)
    paired = jnp.concatenate([key_normed, value_cast], axis=1)
    own_rows = lax.dynamic_slice_in_dim(key_tiles, position * tiles_here, tiles_here, 0)
    blocks = [paired]
    block_ids = [shard_ids(position, frames, tiles_here)]
    for offset in (-1, 1, -2, 2):
        blocks.append(passed_along(paired, "frame", -offset))
        block_ids.append(shard_ids(position + offset, frames, tiles_here))
    far_offsets = []
    stride = 4
    while stride <= frames // 2:
        far_offsets.append(-stride)
        far_offsets.append(stride)
        stride = stride * 2
    for offset in far_offsets:
        source = position + offset
        inside = (source >= 0) & (source < frames)
        wanted = requested(own_rows, source, tiles_here)
        received = passed_along(paired, "frame", -offset)
        blocks.append(received)
        block_ids.append(jnp.where(inside, source * tiles_here + wanted, -2).reshape(1))
    keys_all = jnp.concatenate(blocks, axis=0)
    candidate_ids = jnp.concatenate(block_ids, axis=0)
    candidate_count = candidate_ids.shape[0]
    allowed = jnp.any(own_rows[:, :, None] == candidate_ids[None, None, :], axis=1)
    keys_part = keys_all[:, :columns].reshape(candidate_count, TILE, heads_here, HEAD_DIM)
    values_part = keys_all[:, columns:].reshape(candidate_count, TILE, heads_here, HEAD_DIM)
    queries = query_normed.reshape(tiles_here, TILE, heads_here, HEAD_DIM)

    def one_tile(inputs):
        query_block, usable = inputs
        scores = jnp.einsum(
            "qhd,ckhd->hqck", query_block, keys_part, preferred_element_type=jnp.float32
        ) * HEAD_DIM ** (-0.5)
        scores = jnp.where(usable[None, None, :, None], scores, -jnp.inf)
        highest = jnp.max(scores, axis=(2, 3), keepdims=True)
        raised = jnp.exp(scores - highest)
        softmax_weights = (raised / jnp.sum(raised, axis=(2, 3), keepdims=True)).astype(
            jnp.bfloat16
        )
        combined = jnp.einsum(
            "hqck,ckhd->qhd", softmax_weights, values_part, preferred_element_type=jnp.float32
        )
        return combined.astype(jnp.bfloat16)

    attended = lax.map(one_tile, (queries, allowed))
    return attended.reshape(rows_here, columns)


def solution(mesh):
    return jax.shard_map(
        on_device,
        mesh=mesh,
        in_specs=(
            P("frame", None),
            P("frame", "head"),
            P("frame", "head"),
            P("frame", "head"),
            P("head"),
            P("head"),
            P(),
        ),
        out_specs=P("frame", "head"),
        check_vma=False,
    )
```

profile of v0, /device:TPU:3, one launch (start us, length us, event | category | flops | bytes accessed | tf_op | source)
XLA Modules:
  0.0 518.3 jit_solution(110137075775566827)
XLA Ops:
  6.5 0.0 copy-start
  6.5 0.0 all-gather.4.cloned.1.call-start
  6.5 0.7 all-gather.4.cloned.1.call-update
  7.3 0.0 all-gather.8.cloned.1.call-start
  7.3 0.7 all-gather.8.cloned.1.call-update
  8.0 0.0 all-gather.6.cloned.1.call-start
  8.1 0.7 all-gather.6.cloned.1.call-update
  8.8 1.5 dynamic-slice_reduce_fusion
  12.8 0.1 concatenate.11
  12.9 117.9 %all-gather.4.cloned.1.call-done = bf16[5120,1536]{1,0:T(8,128)(2,1)} async-done(((bf16[320,1536]{1,0:T(8,128)(2,1)}), bf16[5120,1536]{1,0:T(8,128)(2,1)}) %all-gather.4.cloned.1.call-update) | async-done | bytes 15728656 | tf_op jit(solution)/shard_map/all_gather | solution.py:49
  130.7 0.0 copy-done
  130.7 7.8 %multiply_reduce_fusion.1 = (f32[128]{0:T(128)S(1)}, f32[128,1536]{1,0:T(8,128)S(1)}) fusion(bf16[128,5120]{1,0:T(8,128)(2,1)S(1)} %copy-done, bf16[5120,1536]{1,0:T(8,128)(2,1)} %all-gather.4.cloned.1.call-done), kind=kOutput, calls=%fused_computation.15 | convolution fusion | flops 2013659008 | bytes 17826304 | tf_op jit(solution)/shard_map/dot_general | solution.py:18
  138.5 0.0 copy-start.3
  138.5 113.0 %all-gather.8.cloned.1.call-done = bf16[5120,1536]{1,0:T(8,128)(2,1)} async-done(((bf16[320,1536]{1,0:T(8,128)(2,1)}), bf16[5120,1536]{1,0:T(8,128)(2,1)}) %all-gather.8.cloned.1.call-update) | async-done | bytes 15728656 | tf_op jit(solution)/shard_map/all_gather | solution.py:48
  251.5 7.8 %multiply_reduce_fusion = (f32[128]{0:T(128)S(1)}, f32[128,1536]{1,0:T(8,128)S(1)}) fusion(bf16[128,5120]{1,0:T(8,128)(2,1)S(1)} %copy-done, bf16[5120,1536]{1,0:T(8,128)(2,1)} %all-gather.8.cloned.1.call-done), kind=kOutput, calls=%fused_computation.13 | convolution fusion | flops 2013659008 | bytes 17826304 | tf_op jit(solution)/shard_map/dot_general | solution.py:18
  259.3 4.2 all-reduce
  263.5 0.0 copy-done.3
  263.5 0.1 multiply_convert_fusion.1
  263.6 0.0 copy-start.4
  263.7 108.7 %all-gather.6.cloned.1.call-done = bf16[5120,1536]{1,0:T(8,128)(2,1)} async-done(((bf16[320,1536]{1,0:T(8,128)(2,1)}), bf16[5120,1536]{1,0:T(8,128)(2,1)}) %all-gather.6.cloned.1.call-update) | async-done | bytes 15728656 | tf_op jit(solution)/shard_map/all_gather | solution.py:50
  372.4 7.7 %convolution_convert_fusion = bf16[128,1536]{1,0:T(8,128)(2,1)S(1)} fusion(bf16[128,5120]{1,0:T(8,128)(2,1)S(1)} %copy-done, bf16[5120,1536]{1,0:T(8,128)(2,1)} %all-gather.6.cloned.1.call-done), kind=kOutput, calls=%fused_computation.8 | convolution fusion | flops 2013462528 | bytes 17432576 | tf_op jit(solution)/shard_map/dot_general | solution.py:18
  380.0 1.3 pad_maximum_fusion
  381.4 2.3 collective-permute-start
  383.7 0.1 compare_reduce_fusion
  383.8 2.0 collective-permute-start.1
  385.8 2.2 collective-permute-start.2
  388.0 4.1 collective-permute-start.3
  392.1 3.0 collective-permute-start.4
  395.1 0.0 copy-done.4
  395.1 0.1 multiply_convert_fusion
  395.3 0.2 copy.19
  395.5 0.0 collective-permute-done
  395.5 1.3 collective-permute-start.5
  396.8 2.1 constant_dynamic-update-slice_fusion.7
  398.9 3.7 collective-permute-done.1
  402.6 4.5 collective-permute-start.6
  407.1 2.1 constant_dynamic-update-slice_fusion.6
  409.2 27.7 %collective-permute-done.2 = bf16[128,3072]{1,0:T(8,128)(2,1)} collective-permute-done((bf16[128,3072]{1,0:T(8,128)(2,1)}, bf16[128,3072]{1,0:T(8,128)(2,1)}, u32[]{:S(2)}, u32[]{:S(2)}) %collective-permute-start.2) | collective-permute-done | bytes 786464 | tf_op jit(solution)/shard_map/ppermute | solution.py:14
  436.9 1.5 collective-permute-start.7
  438.3 2.1 constant_dynamic-update-slice_fusion.5
  440.4 0.0 collective-permute-done.3
  440.4 2.1 constant_dynamic-update-slice_fusion.4
  442.5 0.0 collective-permute-done.4
  442.5 0.9 constant_dynamic-update-slice_fusion.3
  443.4 0.0 collective-permute-done.5
  443.4 0.9 constant_dynamic-update-slice_fusion.2
  444.4 0.0 collective-permute-done.6
  444.4 1.0 constant_dynamic-update-slice_fusion.1
  445.4 28.5 %collective-permute-done.7 = bf16[128,3072]{1,0:T(8,128)(2,1)S(1)} collective-permute-done((bf16[128,3072]{1,0:T(8,128)(2,1)}, bf16[128,3072]{1,0:T(8,128)(2,1)S(1)}, u32[]{:S(2)}, u32[]{:S(2)}) %collective-permute-start.7) | collective-permute-done | bytes 786464 | tf_op jit(solution)/shard_map/ppermute | solution.py:14
  473.8 0.9 constant_dynamic-update-slice_fusion
  474.8 6.4 %fusion.13 = (bf16[1152,1536]{1,0:T(8,128)(2,1)}, bf16[1152,1536]{1,0:T(8,128)(2,1)}) fusion(bf16[1152,3072]{1,0:T(8,128)(2,1)} %constant_dynamic-update-slice_fusion), kind=kLoop, calls=%fused_computation.35 | loop fusion | bytes 14155776 | tf_op jit(solution)/shard_map/slice | solution.py:82
  481.2 7.3 %reshape.109 = bf16[9,128,12,128]{3,2,1,0:T(8,128)(2,1)} reshape(bf16[1152,1536]{1,0:T(8,128)(2,1)} %get-tuple-element.31) | data formatting | bytes 7077888 | tf_op jit(solution)/shard_map/reshape | solution.py:81
  488.5 3.3 copy.21
  491.8 1.1 fusion.14
  492.9 0.0 copy-start.2
  492.9 1.0 fusion
  493.9 1.5 fusion.1
  495.3 0.5 copy-done.2
  495.8 7.4 %reshape.104 = bf16[9,128,12,128]{3,2,1,0:T(8,128)(2,1)} reshape(bf16[1152,1536]{1,0:T(8,128)(2,1)} %get-tuple-element.30) | data formatting | bytes 7077888 | tf_op jit(solution)/shard_map/reshape | solution.py:82
  503.2 0.0 copy-start.1
  503.2 7.6 %fusion.8 = bf16[12,128,128]{2,1,0:T(8,128)(2,1)S(1)} fusion(f32[12,128,9,128]{1,3,2,0:T(8,128)} %bitcast.32, f32[12,128]{1,0:T(8,128)S(1)} %fusion.1, f32[12,128]{1,0:T(8,128)S(1)} %fusion, pred[9]{0:T(512)(128)(4,1)S(1)} %compare_reduce_fusion, bf16[9,128,12,128]{3,2,1,0:T(8,128)(2,1)} %reshape.104), kind=kOutput, calls=%fused_computation.10 | convolution fusion | flops 462028800 | bytes 11022345 | tf_op jit(solution)/shard_map/while/body/eval_jaxpr/hqck,ckhd->qhd/dot_general | solution.py:96
  510.8 0.9 copy.24
  511.8 0.0 copy-done.1
  (2 shorter events, 0.0 us)
Async XLA Ops:
  6.5 124.2 %copy-start = (bf16[128,5120]{1,0:T(8,128)(2,1)S(1)}, bf16[128,5120]{1,0:T(8,128)(2,1)}, u32[]{:S(2)}) copy-start(bf16[128,5120]{1,0:T(8,128)(2,1)} %param.7) | copy-start | bytes 3932164
  6.5 124.2 %all-gather.4.cloned.1.call-start = ((), (), s32[]{:S(2)}) async-start(), calls=%async_computation | async-start | bytes 16711680 | tf_op jit(solution)/shard_map/all_gather | solution.py:49
  7.3 244.3 %all-gather.8.cloned.1.call-start = ((), (), s32[]{:S(2)}) async-start(), calls=%async_computation.2 | async-start | bytes 16711680 | tf_op jit(solution)/shard_map/all_gather | solution.py:48
  8.0 364.3 %all-gather.6.cloned.1.call-start = ((), (), s32[]{:S(2)}) async-start(), calls=%async_computation.1 | async-start | bytes 16711680 | tf_op jit(solution)/shard_map/all_gather | solution.py:50
  138.5 125.0 %copy-start.3 = (f32[1536]{0:T(1024)S(1)}, f32[1536]{0:T(1024)}, u32[]{:S(2)}) copy-start(f32[1536]{0:T(1024)} %param.12) | copy-start | bytes 18436
  263.6 131.5 %copy-start.4 = (f32[1536]{0:T(1024)S(1)}, f32[1536]{0:T(1024)}, u32[]{:S(2)}) copy-start(f32[1536]{0:T(1024)} %param.11) | copy-start | bytes 18436
  381.4 14.1 %collective-permute-start = (bf16[128,3072]{1,0:T(8,128)(2,1)}, bf16[128,3072]{1,0:T(8,128)(2,1)}, u32[]{:S(2)}, u32[]{:S(2)}) collective-permute-start(bf16[128,3072]{1,0:T(8,128)(2,1)} %get-tuple-element.32), channel_id=1, source_target_pairs={{0,2},{2,4},{4,6},{6,8},{8,10},{10,12},{12,14},{14,16},{16,18},{18... | collective-permute-start | bytes 2359304 | tf_op jit(solution)/shard_map/ppermute | solution.py:14
  383.8 18.8 %collective-permute-start.1 = (bf16[128,3072]{1,0:T(8,128)(2,1)}, bf16[128,3072]{1,0:T(8,128)(2,1)}, u32[]{:S(2)}, u32[]{:S(2)}) collective-permute-start(bf16[128,3072]{1,0:T(8,128)(2,1)} %get-tuple-element.32), channel_id=1, source_target_pairs={{2,0},{4,2},{6,4},{8,6},{10,8},{12,10},{14,12},{16,14},{18,16},{20... | collective-permute-start | bytes 2359304 | tf_op jit(solution)/shard_map/ppermute | solution.py:14
  385.8 51.1 %collective-permute-start.2 = (bf16[128,3072]{1,0:T(8,128)(2,1)}, bf16[128,3072]{1,0:T(8,128)(2,1)}, u32[]{:S(2)}, u32[]{:S(2)}) collective-permute-start(bf16[128,3072]{1,0:T(8,128)(2,1)} %get-tuple-element.32), channel_id=1, source_target_pairs={{0,4},{2,6},{4,8},{6,10},{8,12},{10,14},{12,16},{14,18},{16,20},{1... | collective-permute-start | bytes 2359304 | tf_op jit(solution)/shard_map/ppermute | solution.py:14
  388.0 52.4 %collective-permute-start.3 = (bf16[128,3072]{1,0:T(8,128)(2,1)}, bf16[128,3072]{1,0:T(8,128)(2,1)}, u32[]{:S(2)}, u32[]{:S(2)}) collective-permute-start(bf16[128,3072]{1,0:T(8,128)(2,1)} %get-tuple-element.32), channel_id=1, source_target_pairs={{4,0},{6,2},{8,4},{10,6},{12,8},{14,10},{16,12},{18,14},{20,16},{2... | collective-permute-start | bytes 2359304 | tf_op jit(solution)/shard_map/ppermute | solution.py:14
  392.1 50.4 %collective-permute-start.4 = (bf16[128,3072]{1,0:T(8,128)(2,1)}, bf16[128,3072]{1,0:T(8,128)(2,1)S(1)}, u32[]{:S(2)}, u32[]{:S(2)}) collective-permute-start(bf16[128,3072]{1,0:T(8,128)(2,1)} %get-tuple-element.32), channel_id=1, source_target_pairs={{0,8},{2,10},{4,12},{6,14},{8,16},{10,18},{12,20},{14,22},{16,24},... | collective-permute-start | bytes 2359304 | tf_op jit(solution)/shard_map/ppermute | solution.py:14
  395.5 47.9 %collective-permute-start.5 = (bf16[128,3072]{1,0:T(8,128)(2,1)}, bf16[128,3072]{1,0:T(8,128)(2,1)S(1)}, u32[]{:S(2)}, u32[]{:S(2)}) collective-permute-start(bf16[128,3072]{1,0:T(8,128)(2,1)} %get-tuple-element.32), channel_id=1, source_target_pairs={{8,0},{10,2},{12,4},{14,6},{16,8},{18,10},{20,12},{22,14},{24,16},... | collective-permute-start | bytes 2359304 | tf_op jit(solution)/shard_map/ppermute | solution.py:14
  402.6 41.8 %collective-permute-start.6 = (bf16[128,3072]{1,0:T(8,128)(2,1)}, bf16[128,3072]{1,0:T(8,128)(2,1)S(1)}, u32[]{:S(2)}, u32[]{:S(2)}) collective-permute-start(bf16[128,3072]{1,0:T(8,128)(2,1)} %get-tuple-element.32), channel_id=1, source_target_pairs={{0,16},{2,18},{4,20},{6,22},{8,24},{10,26},{12,28},{14,30},{1,17},... | collective-permute-start | bytes 2359304 | tf_op jit(solution)/shard_map/ppermute | solution.py:14
  436.9 37.0 %collective-permute-start.7 = (bf16[128,3072]{1,0:T(8,128)(2,1)}, bf16[128,3072]{1,0:T(8,128)(2,1)S(1)}, u32[]{:S(2)}, u32[]{:S(2)}) collective-permute-start(bf16[128,3072]{1,0:T(8,128)(2,1)} %get-tuple-element.32), channel_id=1, source_target_pairs={{16,0},{18,2},{20,4},{22,6},{24,8},{26,10},{28,12},{30,14},{17,1},... | collective-permute-start | bytes 2359304 | tf_op jit(solution)/shard_map/ppermute | solution.py:14
  492.9 2.9 copy-start.2
  503.2 8.6 %copy-start.1 = (bf16[128,5120]{1,0:T(8,128)(2,1)S(1)}, bf16[128,5120]{1,0:T(8,128)(2,1)}, u32[]{:S(2)}) copy-start(bf16[128,5120]{1,0:T(8,128)(2,1)} %param.7) | copy-start | bytes 3932164
Sparse Core Ops, SparseCore 0:
  9.7 121.0 all-gather.3
  133.0 118.4 all-gather.7
  253.8 118.4 all-gather.5
where the time goes:
time: 519 us; the launch traced here: 518 us
  waiting for transfers between devices  402 us (77%)
  local copies, waits for them, and re-layouts  38.3 us (7%)
  matrix products  31.9 us (6%)
  starting transfers between devices  21 us (4%)
  between operations  15.9 us (3%)
  other arithmetic  5.63 us (1%)
    all_gather x1, waiting for transfers between devices, on_device(): key_full = add_one(lax.all_gather(w_key, 'frame', axis=0, tiled=True))  118 us
    all_gather x1, waiting for transfers between devices, on_device(): query = add_one(lax.all_gather(w_query, 'frame', axis=0, tiled=True))  113 us
    all_gather x1, waiting for transfers between devices, on_device(): value_full = add_one(lax.all_gather(w_value, 'frame', axis=0, tiled=True))  109 us
    ppermute x8, waiting for transfers between devices, passed_along(): lax.ppermute(value, axis, [(source, source + steps) for source in range(l...  59.8 us
    dot_general x3, matrix products, add_rows(): return jnp.dot(tokens, panel, preferred_element_type=jnp.float32)  23.2 us
    ppermute x8, starting transfers between devices, passed_along(): lax.ppermute(value, axis, [(source, source + steps) for source in range(l...  20.9 us
    unnamed x17, local copies, waits for them, and re-layouts  11.7 us
    reshape x2, local copies, waits for them, and re-layouts, on_device(): keys_all[:, :columns].reshape(candidate_count, TILE, heads_here, HEAD_DIM)  10.6 us
  transfers between devices with their start and end apart: 11, of which 6 were waited for; matrix products, arithmetic and copies ran while one was open for 6% of the time, Pallas kernels for 0%

commit v1 on v0

v1 whole, which is shorter than its diff:
```python
import functools

import jax
import jax.numpy as jnp
from jax import lax
from jax.experimental import pallas as pl
from jax.experimental.pallas import tpu as pltpu
from jax.sharding import PartitionSpec as P

HEAD_DIM = 128
HEADS = 24
TILE = 128
MESH = pl.DeviceIdType.MESH


def plan(frames, heads_here):
    groups = 4 if heads_here % 4 == 0 and frames % 8 == 0 else 1
    return groups, frames // groups


def candidates(frames):
    offsets = [0, 1, -1, 2, -2]
    stride = 4
    while stride < frames // 2:
        offsets += [stride, -stride]
        stride *= 2
    return tuple(offsets + [frames // 2] * (frames // 2 == stride))


def kernel(
    frames, groups, members, sides, offsets,
    tokens, w_query, w_key, w_value, query_gain, key_gain, key_tiles,
    out,
    tok, panel, full, query_normed, keys, values, stat_own, stat_in, sent, landed,
    local_sem, wz_send, wz_recv, tz_send, tz_recv, ty_send, ty_recv,
    wx_send, wx_recv, wc_send, wc_recv, st_send, st_recv,
    kx_send, kx_recv, kc_send, kc_recv, vx_send, vx_recv, vc_send, vc_recv,
    o_send, o_recv,
):
    index = lax.axis_index("frame")
    side = lax.axis_index("head")
    group, member = index // members, index % members
    chip, core = member // 2, member % 2
    chips = members // 2
    rows, width = tokens.shape
    depth = w_query.shape[0]
    part = w_query.shape[1] // groups
    group_depth = depth * members
    share = rows // sides

    def at(to_group, to_member, to_side):
        return (to_group * members + to_member, to_side)

    def other_group(step):
        return (group + step) % groups

    def back_group(step):
        return (group + groups - step) % groups

    def chip_member(step):
        return ((chip + step) % chips) * 2 + core

    def back_member(step):
        return ((chip + chips - step) % chips) * 2 + core

    mate = at(group, chip * 2 + 1 - core, side)

    peers = [mate]
    for step in range(1, chips):
        peers.append(at(group, chip_member(step), side))
    for step in range(groups):
        for turn in range(sides):
            if step or turn:
                peers.append(at(other_group(step), member, (side + turn) % sides))
    barrier = pltpu.get_barrier_semaphore()
    for peer in peers:
        pl.semaphore_signal(barrier, inc=1, device_id=peer, device_id_type=MESH)
    pl.semaphore_wait(barrier, len(peers))

    pending = []

    def send(src, dst, send_sem, recv_sem, device):
        copy = pltpu.make_async_remote_copy(
            src_ref=src, dst_ref=dst, send_sem=send_sem, recv_sem=recv_sem,
            device_id=device, device_id_type=MESH,
        )
        copy.start()
        pending.append(copy)
        return copy

    def member_rows(which):
        return pl.ds(pl.multiple_of(which * depth, depth), depth)

    weights = (w_query, w_key, w_value)

    def columns_of(which):
        return pl.ds(pl.multiple_of(which * part, part), part)

    local = []
    for i, weight in enumerate(weights):
        copy = pltpu.make_async_copy(
            weight.at[:, columns_of(group)],
            panel.at[group, member_rows(member), pl.ds(i * part, part)],
            local_sem.at[i],
        )
        copy.start()
        local.append(copy)
    wz = {}
    for step in range(1, groups):
        for i, weight in enumerate(weights):
            wz[step, i] = send(
                weight.at[:, columns_of(other_group(step))],
                panel.at[group, member_rows(member), pl.ds(i * part, part)],
                wz_send.at[step, i], wz_recv.at[step, i],
                at(other_group(step), member, side),
            )
    own = pltpu.make_async_copy(tokens, tok.at[group], local_sem.at[3])
    own.start()
    half = pl.ds(pl.multiple_of(side * share, share), share)
    tz = {}
    for step in range(1, groups):
        tz[step] = send(
            tokens.at[half], tok.at[group, half], tz_send.at[step], tz_recv.at[step],
            at(other_group(step), member, side),
        )

    for copy in local:
        copy.wait()
    wx, wc = {}, {}

    def spread(step):
        block = panel.at[back_group(step), member_rows(member)]
        for hop in range(1, chips):
            wx[step, hop] = send(
                block, block, wx_send.at[step, hop], wx_recv.at[step, hop],
                at(group, chip_member(hop), side),
            )
        wc[step, 0] = send(block, block, wc_send.at[step, 0], wc_recv.at[step, 0], mate)

    def relay(step):
        for hop in range(1, chips):
            wx[step, hop].wait_recv()
            block = panel.at[back_group(step), member_rows(back_member(hop))]
            wc[step, hop] = send(
                block, block, wc_send.at[step, hop], wc_recv.at[step, hop], mate
            )

    spread(0)
    for step in range(1, groups):
        for i in range(len(weights)):
            wz[step, i].wait_recv()
        spread(step)
        relay(step - 1)
    ty = {}
    for step in range(1, groups):
        tz[step].wait_recv()
        block = tok.at[back_group(step), half]
        for turn in range(1, sides):
            ty[step, turn] = send(
                block, block, ty_send.at[step, turn], ty_recv.at[step, turn],
                at(group, member, (side + turn) % sides),
            )
    relay(groups - 1)
    for step in range(groups):
        for hop in range(chips):
            wc[step, hop].wait_recv()
    own.wait()

    def project(which):
        @pl.loop(0, 3)
        def _(i):
            cols = pl.ds(pl.multiple_of(i * part, part), part)
            total = jnp.zeros((rows, part), jnp.float32)
            for g in range(groups):
                total += jnp.dot(
                    tok[which, :, g * group_depth:(g + 1) * group_depth],
                    panel[g, :, cols],
                    preferred_element_type=jnp.float32,
                )
            full[which, :, cols] = total

    project(group)
    for step in range(1, groups):
        for turn in range(1, sides):
            ty[step, turn].wait_recv()
        project(back_group(step))

    def gathered(buffer, x_send, x_recv, c_send, c_recv):
        block = buffer.at[member]
        across = [
            send(block, block, x_send.at[hop], x_recv.at[hop], at(group, chip_member(hop), side))
            for hop in range(1, chips)
        ]
        beside = [send(block, block, c_send.at[0], c_recv.at[0], mate)]

        def finish():
            for hop in range(1, chips):
                across[hop - 1].wait_recv()
                come = buffer.at[back_member(hop)]
                beside.append(send(come, come, c_send.at[hop], c_recv.at[hop], mate))
            return beside

        return finish

    first_row = lax.broadcasted_iota(jnp.int32, (8, TILE), 0) < 4
    for g in range(groups):
        spot = slice(g * rows, (g + 1) * rows)
        query = full[g, :, 0:part]
        key = full[g, :, part:2 * part]
        values[member, spot, :] = full[g, :, 2 * part:3 * part].astype(jnp.bfloat16)
        sums = []
        for value in (query, key):
            column = jnp.sum(value * value, axis=1, keepdims=True)
            sums.append(jnp.broadcast_to(column, (rows, TILE)).T[0:8, :])
        stat_own[:, spot] = jnp.where(first_row, sums[0], sums[1])
    st = []
    for step in range(groups):
        for turn in range(sides):
            if step or turn:
                slot = step * sides + turn
                st.append(send(
                    stat_own, stat_in.at[slot], st_send.at[slot], st_recv.at[slot],
                    at(other_group(step), member, (side + turn) % sides),
                ))
    finish_values = gathered(values, vx_send, vx_recv, vc_send, vc_recv)
    totals = stat_own[...]
    for slot in range(1, groups * sides):
        st[slot - 1].wait_recv()
        totals = totals + stat_in[slot]
    scales = lax.rsqrt(totals / (HEADS * HEAD_DIM) + 1e-06)
    q_gain = query_gain[pl.ds(group, 1), :]
    k_gain = key_gain[pl.ds(group, 1), :]

    def normed(value, row, gain):
        column = jnp.broadcast_to(row, (TILE, TILE)).T
        column = jnp.concatenate([column] * (part // TILE), axis=1)
        return (value * column * gain).astype(jnp.bfloat16)

    for g in range(groups):
        spot = slice(g * rows, (g + 1) * rows)
        keys[member, spot, :] = normed(full[g, :, part:2 * part], scales[4:5, spot], k_gain)
    finish_keys = gathered(keys, kx_send, kx_recv, kc_send, kc_recv)
    for g in range(groups):
        spot = slice(g * rows, (g + 1) * rows)
        query_normed[g] = normed(full[g, :, 0:part], scales[0:1, spot], q_gain)
    values_beside = finish_values()
    keys_beside = finish_keys()
    for copy in values_beside + keys_beside:
        copy.wait_recv()

    def attend(which, target):
        tile = which * members + member

        named = key_tiles[pl.ds(tile, 1), :]
        places, usable = [], []
        for offset in offsets:
            other = tile + offset
            place = (other + frames) % frames
            wanted = place if offset == frames // 2 else jnp.where(other < 0, -2, other)
            places.append((place // members, place % members))
            hits = jnp.where(named == wanted, 1.0, 0.0)
            usable.append(jnp.broadcast_to(jnp.max(hits, axis=1, keepdims=True), (TILE, TILE)))

        @pl.loop(0, part // HEAD_DIM)
        def _(head):
            cols = pl.ds(pl.multiple_of(head * HEAD_DIM, HEAD_DIM), HEAD_DIM)
            query = query_normed[which, :, cols]
            scores, parts = [], []
            for (other_part, other_member), use in zip(places, usable):
                spot = pl.ds(pl.multiple_of(other_part * TILE, TILE), TILE)
                key = keys[other_member, spot, cols]
                parts.append(values[other_member, spot, cols])
                score = lax.dot_general(
                    query, key, (((1,), (1,)), ((), ())), preferred_element_type=jnp.float32
                ) * HEAD_DIM ** (-0.5)
                scores.append(jnp.where(use > 0.5, score, -jnp.inf))
            scores = jnp.concatenate(scores, axis=1)
            highest = jnp.max(scores, axis=1, keepdims=True)
            raised = jnp.exp(scores - highest)
            softmax_weights = (raised / jnp.sum(raised, axis=1, keepdims=True)).astype(jnp.bfloat16)
            combined = jnp.dot(
                softmax_weights, jnp.concatenate(parts, axis=0), preferred_element_type=jnp.float32
            )
            target[:, cols] = combined.astype(jnp.bfloat16)

    outs = []
    for step in range(1, groups):
        attend(other_group(step), sent.at[step])
        outs.append(send(
            sent.at[step], landed.at[group], o_send.at[step], o_recv.at[step],
            at(other_group(step), member, side),
        ))
    attend(group, landed.at[group])
    for copy in outs:
        copy.wait_recv()
    for g in range(groups):
        out[:, g * part:(g + 1) * part] = landed[g]
    for copy in pending:
        copy.wait_send()


def on_device(tokens, w_query, w_key, w_value, query_gain, key_gain, key_tiles):
    frames, sides = lax.axis_size("frame"), lax.axis_size("head")
    rows, width = tokens.shape
    depth, columns = w_query.shape
    groups, members = plan(frames, columns // HEAD_DIM)
    chips = members // 2
    part = columns // groups
    dma = pltpu.SemaphoreType.DMA
    bf16, f32 = jnp.bfloat16, jnp.float32
    whole = pl.BlockSpec(memory_space=pltpu.VMEM)
    far = pl.BlockSpec(memory_space=pl.ANY)
    return pl.pallas_call(
        functools.partial(kernel, frames, groups, members, sides, candidates(frames)),
        out_shape=jax.ShapeDtypeStruct((rows, columns), bf16),
        in_specs=[far, far, far, far, whole, whole, whole],
        out_specs=whole,
        scratch_shapes=[
            pltpu.VMEM((groups, rows, width), bf16),
            pltpu.VMEM((groups, depth * members, 3 * part), bf16),
            pltpu.VMEM((groups, rows, 3 * part), f32),
            pltpu.VMEM((groups, rows, part), bf16),
            pltpu.VMEM((members, groups * rows, part), bf16),
            pltpu.VMEM((members, groups * rows, part), bf16),
            pltpu.VMEM((8, groups * rows), f32),
            pltpu.VMEM((groups * sides, 8, groups * rows), f32),
            pltpu.VMEM((groups, rows, part), bf16),
            pltpu.VMEM((groups, rows, part), bf16),
            dma((4,)),
            dma((groups, 3)), dma((groups, 3)),
            dma((groups,)), dma((groups,)),
            dma((groups, sides)), dma((groups, sides)),
            dma((groups, chips)), dma((groups, chips)),
            dma((groups, chips)), dma((groups, chips)),
            dma((groups * sides,)), dma((groups * sides,)),
            dma((chips,)), dma((chips,)), dma((chips,)), dma((chips,)),
            dma((chips,)), dma((chips,)), dma((chips,)), dma((chips,)),
            dma((groups,)), dma((groups,)),
        ],
        compiler_params=pltpu.CompilerParams(
            collective_id=0, has_side_effects=True, vmem_limit_bytes=48 * 1024 * 1024
        ),
        cost_estimate=pl.CostEstimate(
            flops=2 * rows * width * 3 * columns, bytes_accessed=20 * 1024 * 1024,
            transcendentals=0,
        ),
    )(
        tokens, w_query, w_key, w_value,
        query_gain.reshape(groups, part), key_gain.reshape(groups, part), key_tiles,
    )


def solution(mesh):
    return jax.shard_map(
        on_device,
        mesh=mesh,
        in_specs=(
            P("frame", None),
            P("frame", "head"),
            P("frame", "head"),
            P("frame", "head"),
            P("head"),
            P("head"),
            P(),
        ),
        out_specs=P("frame", "head"),
        check_vma=False,
    )
```

time: 519 us -> 198 us (0.38)
  waiting for transfers between devices: 402 us -> 0 us
  Pallas kernels: 0 us -> 188 us
  matrix products: 31.9 us -> 0 us
  local copies, waits for them, and re-layouts: 38.3 us -> 7.83 us
  starting transfers between devices: 21 us -> 0 us
  between operations: 15.9 us -> 0.01 us
  other arithmetic: 5.63 us -> 0 us
    all_gather x3 -> x0, waiting for transfers between devices: 340 us -> none  [the longest x1 118 us: on_device(): key_full = add_one(lax.all_gather(w_key, 'frame', axis=0, tiled=True))]
    pallas_call x0 -> x1, Pallas kernels: none -> 188 us  [on_device(): pl.pallas_call(functools.partial(kernel, frames, groups, members, sides,...]
    ppermute x8 -> x0, waiting for transfers between devices: 59.8 us -> none  [passed_along(): lax.ppermute(value, axis, [(source, source + steps) for source in range(l...]
    dot_general x4 -> x0, matrix products: 30.8 us -> none  [the longest x3 23.2 us: add_rows(): return jnp.dot(tokens, panel, preferred_element_type=jnp.float32)]
    ppermute x8 -> x0, starting transfers between devices: 20.9 us -> none  [passed_along(): lax.ppermute(value, axis, [(source, source + steps) for source in range(l...]
    reshape x4 -> x2, local copies, waits for them, and re-layouts: 18.9 us -> 1.41 us  [the longest x1 0.7 us: on_device(): query_gain.reshape(groups, part)]
    slice x1 -> x0, local copies, waits for them, and re-layouts: 6.41 us -> none  [on_device(): keys_all[:, columns:].reshape(candidate_count, TILE, heads_here, HEAD_DIM)]
    unnamed x17 -> x10, local copies, waits for them, and re-layouts: 11.7 us -> 6.42 us
  transfers between devices with their start and end apart: 11 -> 0, of which waited for: 6 -> 0; matrix products, arithmetic and copies ran while one was open for 6% -> 0% of each run, Pallas kernels for 0% -> 0%
where the time goes in v1:
time: 198 us; the launch traced here: 195 us
  Pallas kernels  188 us (95%)
  local copies, waits for them, and re-layouts  7.83 us (4%)
    pallas_call x1, Pallas kernels, on_device(): pl.pallas_call(functools.partial(kernel, frames, groups, members, sides,...  188 us
    unnamed x10, local copies, waits for them, and re-layouts  6.42 us

profile of v1, /device:TPU:3, one launch (start us, length us, event | category | flops | bytes accessed | tf_op | source)
XLA Modules:
  0.0 195.4 jit_solution(2999546693345651147)
XLA Ops:
  0.0 0.7 reshape.6.query_gain
  0.7 0.7 reshape.7.key_gain
  1.4 0.8 copy.8.key_tiles
  2.2 0.0 copy-start
  2.2 1.3 copy-done
  3.5 0.0 copy-start.1
  3.5 1.2 copy-done.1
  4.7 0.0 copy-start.2
  4.7 1.2 copy-done.2
  5.9 0.0 copy-start.3
  5.9 1.2 copy-done.3
  7.1 187.5 %shard_map.73 = bf16[128,1536]{1,0:T(8,128)(2,1)S(1)} custom-call(bf16[128,5120]{1,0:T(8,128)(2,1)S(1)} %copy-done, bf16[320,1536]{1,0:T(8,128)(2,1)S(1)} %copy-done.1, bf16[320,1536]{1,0:T(8,128)(2,1)S(1)} %copy-done.2, bf16[320,1536]{1,0:T(8,128)(2,1)S(1)} %copy-done.3, f32[4,384]{1,0:T(4,128)S(1)} %reshape.6.query_gain, f32[4,384]{1,0:T(4,128)S(1)} %reshape.7.key_gain, ...), custom_call_target="tpu_custom_call" | custom-call | flops 6039797760 | bytes 20971520 | tf_op jit(solution)/shard_map/pallas_call | solution.py:313
  194.6 0.7 copy.10
Async XLA Ops:
  2.2 1.3 copy-start
  3.5 1.2 copy-start.1
  4.7 1.2 copy-start.2
  5.9 1.2 copy-start.3

commit v2 on v1

--- a/solution.py
+++ b/solution.py
@@ -117,12 +117,40 @@
     own = pltpu.make_async_copy(tokens, tok.at[group], local_sem.at[3])
     own.start()
     half = pl.ds(pl.multiple_of(side * share, share), share)
-    tz = {}
-    for step in range(1, groups):
-        tz[step] = send(
-            tokens.at[half], tok.at[group, half], tz_send.at[step], tz_recv.at[step],
-            at(other_group(step), member, side),
+
+    def has(which):
+        return (which >= 0) & (which < groups)
+
+    def tok_half(source):
+        return tok.at[source, half]
+
+    def hop_copy(way, k):
+        source, to = group - way * k, group + way
+        slot = (1 - way) // 2 * groups + k
+        src = tokens.at[half] if k == 0 else tok_half(source)
+        return has(source) & has(to), pltpu.make_async_remote_copy(
+            src_ref=src, dst_ref=tok_half(source), send_sem=tz_send.at[slot],
+            recv_sem=tz_recv.at[slot], device_id=at(to, member, side), device_id_type=MESH,
         )
+
+    def swap_copies(way, k):
+        slot = (1 - way) // 2 * groups + k
+        block = tok_half(group - way * (k + 1))
+        return [
+            pltpu.make_async_remote_copy(
+                src_ref=block, dst_ref=block, send_sem=ty_send.at[slot, turn],
+                recv_sem=ty_recv.at[slot, turn],
+                device_id=at(group, member, (side + turn) % sides), device_id_type=MESH,
+            )
+            for turn in range(1, sides)
+        ]
+
+    ways = [(way, k) for k in range(groups - 1) for way in (1, -1)]
+
+    def start_hop(way, k):
+        @pl.when(hop_copy(way, k)[0])
+        def _():
+            hop_copy(way, k)[1].start()
 
     for copy in local:
         copy.wait()
@@ -151,16 +179,22 @@
             wz[step, i].wait_recv()
         spread(step)
         relay(step - 1)
-    ty = {}
-    for step in range(1, groups):
-        tz[step].wait_recv()
-        block = tok.at[back_group(step), half]
-        for turn in range(1, sides):
-            ty[step, turn] = send(
-                block, block, ty_send.at[step, turn], ty_recv.at[step, turn],
-                at(group, member, (side + turn) % sides),
-            )
+    for copy in wz.values():
+        copy.wait_send()
+        pending.remove(copy)
+    if groups > 1:
+        start_hop(1, 0)
+        start_hop(-1, 0)
     relay(groups - 1)
+    for way, k in ways:
+        @pl.when(has(group - way * (k + 1)))
+        def _(way=way, k=k):
+            hop_copy(way, k)[1].wait_recv()
+            if k + 1 < groups - 1:
+                start_hop(way, k + 1)
+            for copy in swap_copies(way, k):
+                copy.start()
+
     for step in range(groups):
         for hop in range(chips):
             wc[step, hop].wait_recv()
@@ -180,10 +214,12 @@
             full[which, :, cols] = total
 
     project(group)
-    for step in range(1, groups):
-        for turn in range(1, sides):
-            ty[step, turn].wait_recv()
-        project(back_group(step))
+    for way, k in ways:
+        @pl.when(has(group - way * (k + 1)))
+        def _(way=way, k=k):
+            for copy in swap_copies(way, k):
+                copy.wait_recv()
+            project(group - way * (k + 1))
 
     def gathered(buffer, x_send, x_recv, c_send, c_recv):
         block = buffer.at[member]
@@ -261,9 +297,8 @@
             hits = jnp.where(named == wanted, 1.0, 0.0)
             usable.append(jnp.broadcast_to(jnp.max(hits, axis=1, keepdims=True), (TILE, TILE)))
 
-        @pl.loop(0, part // HEAD_DIM)
-        def _(head):
-            cols = pl.ds(pl.multiple_of(head * HEAD_DIM, HEAD_DIM), HEAD_DIM)
+        for head in range(part // HEAD_DIM):
+            cols = pl.ds(head * HEAD_DIM, HEAD_DIM)
             query = query_normed[which, :, cols]
             scores, parts = [], []
             for (other_part, other_member), use in zip(places, usable):
@@ -297,6 +332,15 @@
         out[:, g * part:(g + 1) * part] = landed[g]
     for copy in pending:
         copy.wait_send()
+    for way, k in ways:
+        @pl.when(hop_copy(way, k)[0])
+        def _(way=way, k=k):
+            hop_copy(way, k)[1].wait_send()
+
+        @pl.when(has(group - way * (k + 1)))
+        def _(way=way, k=k):
+            for copy in swap_copies(way, k):
+                copy.wait_send()
 
 
 def on_device(tokens, w_query, w_key, w_value, query_gain, key_gain, key_tiles):
@@ -328,8 +372,8 @@
             pltpu.VMEM((groups, rows, part), bf16),
             dma((4,)),
             dma((groups, 3)), dma((groups, 3)),
-            dma((groups,)), dma((groups,)),
-            dma((groups, sides)), dma((groups, sides)),
+            dma((2 * groups,)), dma((2 * groups,)),
+            dma((2 * groups, sides)), dma((2 * groups, sides)),
             dma((groups, chips)), dma((groups, chips)),
             dma((groups, chips)), dma((groups, chips)),
             dma((groups * sides,)), dma((groups * sides,)),

time: 198 us -> 183 us (0.924)
  Pallas kernels: 188 us -> 174 us
    pallas_call x1, Pallas kernels: 188 us -> 174 us  [on_device(): pl.pallas_call(functools.partial(kernel, frames, groups, members, sides,...]
where the time goes in v2:
time: 183 us; the launch traced here: 181 us
  Pallas kernels  174 us (95%)
  local copies, waits for them, and re-layouts  7.83 us (4%)
    pallas_call x1, Pallas kernels, on_device(): pl.pallas_call(functools.partial(kernel, frames, groups, members, sides,...  174 us
    unnamed x10, local copies, waits for them, and re-layouts  6.42 us

profile of v2, /device:TPU:3, one launch (start us, length us, event | category | flops | bytes accessed | tf_op | source)
XLA Modules:
  0.0 181.4 jit_solution(8227757773932307323)
XLA Ops:
  0.0 0.7 reshape.6.query_gain
  0.7 0.7 reshape.7.key_gain
  1.4 0.8 copy.8.key_tiles
  2.2 0.0 copy-start
  2.2 1.3 copy-done
  3.5 0.0 copy-start.1
  3.5 1.2 copy-done.1
  4.7 0.0 copy-start.2
  4.7 1.2 copy-done.2
  5.9 0.0 copy-start.3
  5.9 1.2 copy-done.3
  7.1 173.5 %shard_map.73 = bf16[128,1536]{1,0:T(8,128)(2,1)S(1)} custom-call(bf16[128,5120]{1,0:T(8,128)(2,1)S(1)} %copy-done, bf16[320,1536]{1,0:T(8,128)(2,1)S(1)} %copy-done.1, bf16[320,1536]{1,0:T(8,128)(2,1)S(1)} %copy-done.2, bf16[320,1536]{1,0:T(8,128)(2,1)S(1)} %copy-done.3, f32[4,384]{1,0:T(4,128)S(1)} %reshape.6.query_gain, f32[4,384]{1,0:T(4,128)S(1)} %reshape.7.key_gain, ...), custom_call_target="tpu_custom_call" | custom-call | flops 6039797760 | bytes 20971520 | tf_op jit(solution)/shard_map/pallas_call | solution.py:357
  180.6 0.7 copy.10
Async XLA Ops:
  2.2 1.3 copy-start
  3.5 1.2 copy-start.1
  4.7 1.2 copy-start.2
  5.9 1.2 copy-start.3

commit v3 on v2

--- a/solution.py
+++ b/solution.py
@@ -175,16 +175,13 @@
 
     spread(0)
     for step in range(1, groups):
+        if step == groups - 1:
+            start_hop(1, 0)
+            start_hop(-1, 0)
         for i in range(len(weights)):
             wz[step, i].wait_recv()
         spread(step)
         relay(step - 1)
-    for copy in wz.values():
-        copy.wait_send()
-        pending.remove(copy)
-    if groups > 1:
-        start_hop(1, 0)
-        start_hop(-1, 0)
     relay(groups - 1)
     for way, k in ways:
         @pl.when(has(group - way * (k + 1)))

time: 183 us -> 181 us (0.989)
  Pallas kernels: 174 us -> 172 us
where the time goes in v3:
time: 181 us; the launch traced here: 180 us
  Pallas kernels  172 us (95%)
  local copies, waits for them, and re-layouts  7.83 us (4%)
    pallas_call x1, Pallas kernels, on_device(): pl.pallas_call(functools.partial(kernel, frames, groups, members, sides,...  172 us
    unnamed x10, local copies, waits for them, and re-layouts  6.42 us

profile of v3, /device:TPU:3, one launch (start us, length us, event | category | flops | bytes accessed | tf_op | source)
XLA Modules:
  0.0 180.0 jit_solution(7255066409664936301)
XLA Ops:
  0.0 0.7 reshape.6.query_gain
  0.7 0.7 reshape.7.key_gain
  1.4 0.8 copy.8.key_tiles
  2.2 0.0 copy-start
  2.2 1.3 copy-done
  3.5 0.0 copy-start.1
  3.5 1.2 copy-done.1
  4.7 0.0 copy-start.2
  4.7 1.2 copy-done.2
  5.9 0.0 copy-start.3
  5.9 1.2 copy-done.3
  7.1 172.2 %shard_map.73 = bf16[128,1536]{1,0:T(8,128)(2,1)S(1)} custom-call(bf16[128,5120]{1,0:T(8,128)(2,1)S(1)} %copy-done, bf16[320,1536]{1,0:T(8,128)(2,1)S(1)} %copy-done.1, bf16[320,1536]{1,0:T(8,128)(2,1)S(1)} %copy-done.2, bf16[320,1536]{1,0:T(8,128)(2,1)S(1)} %copy-done.3, f32[4,384]{1,0:T(4,128)S(1)} %reshape.6.query_gain, f32[4,384]{1,0:T(4,128)S(1)} %reshape.7.key_gain, ...), custom_call_target="tpu_custom_call" | custom-call | flops 6039797760 | bytes 20971520 | tf_op jit(solution)/shard_map/pallas_call | solution.py:354
  179.3 0.7 copy.10
Async XLA Ops:
  2.2 1.3 copy-start
  3.5 1.2 copy-start.1
  4.7 1.2 copy-start.2
  5.9 1.2 copy-start.3
